TPU v7x, 32 devices: a whole 2x2x4 slice. The times are simulated.
32 devices in a mesh: roll: 16 (over z, y, core), seq: 2 (over x).
Axes of the slice: x: 2, y: 2, z: 4, core: 2. Of those that a mesh axis runs over, the one named last changes fastest.
Arguments:
- queries: bfloat16 [8192, 3072], P(('roll', 'seq')), parts along dimension 0, may hold values from -7.5 to 7.5
- keys_in: bfloat16 [8192, 3072], P(('roll', 'seq')), parts along dimension 0, may hold values from -7.5 to 7.5
- values_in: bfloat16 [8192, 3072], P(('roll', 'seq')), parts along dimension 0, may hold values from -6 to 6
- latent_proj: bfloat16 [3072, 64], replicated, may hold values from -3 to 3
- conv_weight: bfloat16 [432, 512], replicated, may hold values from -0.3125 to 0.3125
- conv_bias: float32 [512], replicated, may hold values from -3 to 3
- pool_weight: float32 [2, 2, 8, 64], P('seq'), may hold values from -5 to 5
- tile_block: int32 [128], P('roll'), parts along dimension 0, may hold values from 0 to 7, each once
- owner_slot: int32 [64], P('roll'), parts along dimension 0, may hold values from 0 to 3, each once
Outputs:
- decoded: bfloat16 [32, 2, 8, 64, 512], P(('roll', 'seq')), parts along dimension 0
- policy_features: float32 [64, 512], P(('roll', 'seq')), parts along dimension 0
There are 16 independent parts, one for each index of `roll`. A program takes and returns all parts, laid end to end along the dimension named above; an argument that names none is the same for every part. Nothing has to cross between parts.
Inputs may be any that keep to these rules, and one draw needn't show every extreme that they name: `tile_block`: each piece index once. `owner_slot`: each row once.
All inputs are finite; a program needn't handle non-finite values.
Results may differ from a plain program's by a relative error of at most 0.013.
Values may be sent and summed in bfloat16 or wider, within the bound.
A program may use at most 64 MiB of HBM per device.

v0:
```python
import math

import jax
import jax.numpy as jnp
from jax import lax
from jax.sharding import PartitionSpec as P

H = 24
HD = 128
LC = 16
CO = 512
S_DEV = 256
RT = 4
WT = 32
TR = 2
BPD = 2
FT = 2
RL = 8
COLS = 64


def shifted(array, axis, by):
    length = lax.axis_size(axis)
    pairs = [(i, i + by) for i in range(length) if 0 <= i + by < length]
    return lax.ppermute(array, axis, pairs)


def swapped(array, axis, bit):
    return lax.ppermute(array, axis, [(i, i ^ 1 << bit) for i in range(lax.axis_size(axis))])


def heads_attention(query_all, key_all, value_all):
    length = query_all.shape[0]
    block_rows = min(512, length)
    score_scale = 1.0 / math.sqrt(query_all.shape[2])
    query_blocks = query_all.reshape(
        length // block_rows, block_rows, query_all.shape[1], query_all.shape[2]
    )

    def one_block(query_part):
        scores = (
            jnp.einsum("qhd,khd->hqk", query_part, key_all, preferred_element_type=jnp.float32)
            * score_scale
        )
        expo = jnp.exp(scores - jnp.max(scores, axis=-1, keepdims=True))
        totals = jnp.sum(expo, axis=-1, keepdims=True)
        mixed = jnp.einsum(
            "hqk,khd->qhd", expo.astype(jnp.bfloat16), value_all, preferred_element_type=jnp.float32
        )
        return (mixed / jnp.transpose(totals, (1, 0, 2))).astype(jnp.bfloat16)

    return lax.map(one_block, query_blocks).reshape(length, query_all.shape[1], query_all.shape[2])


def window_columns(volume):
    frame_count = volume.shape[0] - 2
    row_count = volume.shape[1] - 2
    col_count = volume.shape[2] - 2
    pieces = [
        volume[a : a + frame_count, b : b + row_count, c : c + col_count]
        for a in range(3)
        for b in range(3)
        for c in range(3)
    ]
    return jnp.concatenate(pieces, axis=-1).reshape(
        frame_count * row_count * col_count, 27 * volume.shape[3]
    )


def local(
    queries,
    keys_in,
    values_in,
    latent_proj,
    conv_weight,
    conv_bias,
    pool_weight,
    tile_block,
    owner_slot,
):
    group_count = lax.axis_size("seq")
    my_index = lax.axis_index("seq")
    seq_len = S_DEV * group_count
    heads_dev = H // group_count
    quarter = S_DEV // 4

    def to_groups(matrix):
        return matrix.reshape(S_DEV, group_count, heads_dev, HD)

    query_all = lax.all_to_all(to_groups(queries), "seq", split_axis=1, concat_axis=0, tiled=True)
    key_all = lax.all_to_all(to_groups(keys_in), "seq", split_axis=1, concat_axis=0, tiled=True)
    value_all = lax.all_to_all(to_groups(values_in), "seq", split_axis=1, concat_axis=0, tiled=True)
    mixed = heads_attention(query_all[:, 0], key_all[:, 0], value_all[:, 0])[:, None]
    flat_heads = mixed.reshape(seq_len, heads_dev * HD)
    ordered = flat_heads.reshape(4 * group_count, quarter, heads_dev * HD)[tile_block]
    ordered = ordered.reshape(seq_len, 1, heads_dev, HD)
    returned = lax.all_to_all(ordered, "seq", split_axis=0, concat_axis=1, tiled=True)
    tile_heads = returned.reshape(S_DEV, H * HD)
    latent = jnp.dot(tile_heads, latent_proj, preferred_element_type=jnp.float32).astype(
        jnp.bfloat16
    )
    tile_latent = (
        latent.reshape(FT, RT, WT, 2, 2, LC).transpose(0, 1, 3, 2, 4, 5).reshape(FT, RL, COLS * LC)
    )
    earlier = shifted(tile_latent, "seq", TR)
    extended = jnp.concatenate([earlier, tile_latent], axis=0)
    band_row = my_index % TR
    upper_band = band_row == 0
    outgoing = jnp.where(upper_band, extended[:, RL - 1 :], extended[:, :1])
    incoming = swapped(outgoing, "seq", 0)
    above = jnp.where(upper_band, jnp.zeros_like(incoming), incoming)
    below = jnp.where(upper_band, incoming, jnp.zeros_like(incoming))
    volume = jnp.concatenate([above, extended, below], axis=1).reshape(FT + 2, RL + 2, COLS, LC)
    volume = jnp.pad(volume, ((0, 0), (0, 0), (1, 1), (0, 0)))
    pre_act = (
        jnp.dot(window_columns(volume), conv_weight, preferred_element_type=jnp.float32) + conv_bias
    )
    decoded = pre_act.astype(jnp.bfloat16).reshape(1, FT, RL, COLS, CO)
    block_count = BPD * group_count
    band_voxels = group_count // TR * FT * TR * RL * (COLS // block_count)
    weighted = jax.nn.silu(pre_act).reshape(FT, RL, COLS, CO) * pool_weight[0][..., None]
    pooled_term = jnp.sum(weighted, axis=(0, 1)).reshape(block_count, COLS // block_count, CO).sum(
        axis=1
    ) / math.sqrt(band_voxels)
    total_pooled = lax.psum(pooled_term.astype(jnp.bfloat16), "seq").astype(jnp.float32)
    wanted_rows = my_index * BPD + jnp.arange(BPD, dtype=jnp.int32)
    chooser = (owner_slot[None, :] == wanted_rows[:, None]).astype(jnp.float32)
    policy = jnp.dot(
        chooser, total_pooled, precision=lax.Precision.HIGHEST, preferred_element_type=jnp.float32
    )
    return (decoded, policy)


def solution(mesh):
    placed = (
        P(("roll", "seq"), None),
        P(("roll", "seq"), None),
        P(("roll", "seq"), None),
        P(),
        P(),
        P(),
        P("seq", None, None, None),
        P("roll"),
        P("roll"),
    )
    return jax.shard_map(
        local,
        mesh=mesh,
        in_specs=placed,
        out_specs=(P(("roll", "seq"), None, None, None, None), P(("roll", "seq"), None)),
        check_vma=False,
    )
```

profile of v0, /device:TPU:0, one launch (start us, length us, event | category | flops | bytes accessed | tf_op | source)
XLA Modules:
  0.0 149.0 jit_solution(7226683860920676118)
XLA Ops:
  0.6 0.0 copy-start
  0.6 2.7 %copy.64 = bf16[256,3072]{0,1:T(8,128)(2,1)} copy(bf16[256,3072]{1,0:T(8,128)(2,1)} %param.9) | data formatting | bytes 3145728 | tf_op args[0]
  3.3 4.2 %all-to-all-start = ((bf16[256,2,12,128]{0,3,2,1:T(8,128)(2,1)}), bf16[256,2,12,128]{0,3,2,1:T(8,128)(2,1)S(1)}, u32[]{:S(2)}, u32[]{:S(2)}) async-start(bf16[256,2,12,128]{0,3,2,1:T(8,128)(2,1)} %bitcast.52), calls=%async_computation | async-start | bytes 3145728 | tf_op jit(solution)/shard_map/all_to_all | solution.py:90
  7.5 2.6 %copy.66 = bf16[256,3072]{0,1:T(8,128)(2,1)} copy(bf16[256,3072]{1,0:T(8,128)(2,1)} %param.10) | data formatting | bytes 3145728 | tf_op args[1]
  10.1 17.6 %all-to-all-done = bf16[256,2,12,128]{0,3,2,1:T(8,128)(2,1)S(1)} async-done(((bf16[256,2,12,128]{0,3,2,1:T(8,128)(2,1)}), bf16[256,2,12,128]{0,3,2,1:T(8,128)(2,1)S(1)}, u32[]{:S(2)}, u32[]{:S(2)}) %all-to-all-start) | async-done | bytes 1572896 | tf_op jit(solution)/shard_map/all_to_all | solution.py:90
  27.6 4.6 %all-to-all-start.1 = ((bf16[256,2,12,128]{0,3,2,1:T(8,128)(2,1)}), bf16[256,2,12,128]{0,3,2,1:T(8,128)(2,1)}, u32[]{:S(2)}, u32[]{:S(2)}) async-start(bf16[256,2,12,128]{0,3,2,1:T(8,128)(2,1)} %bitcast.51), calls=%async_computation.1 | async-start | bytes 3145728 | tf_op jit(solution)/shard_map/all_to_all | solution.py:91
  32.3 2.6 %copy.68 = bf16[256,3072]{0,1:T(8,128)(2,1)} copy(bf16[256,3072]{1,0:T(8,128)(2,1)} %param.11) | data formatting | bytes 3145728 | tf_op args[2]
  34.9 0.0 copy-start.6
  34.9 16.4 %all-to-all-done.1 = bf16[256,2,12,128]{0,3,2,1:T(8,128)(2,1)} async-done(((bf16[256,2,12,128]{0,3,2,1:T(8,128)(2,1)}), bf16[256,2,12,128]{0,3,2,1:T(8,128)(2,1)}, u32[]{:S(2)}, u32[]{:S(2)}) %all-to-all-start.1) | async-done | bytes 1572896 | tf_op jit(solution)/shard_map/all_to_all | solution.py:91
  51.3 4.6 %all-to-all-start.2 = ((bf16[256,2,12,128]{0,3,2,1:T(8,128)(2,1)}), bf16[256,2,12,128]{0,3,2,1:T(8,128)(2,1)}, u32[]{:S(2)}, u32[]{:S(2)}) async-start(bf16[256,2,12,128]{0,3,2,1:T(8,128)(2,1)} %bitcast.50), calls=%async_computation.2 | async-start | bytes 3145728 | tf_op jit(solution)/shard_map/all_to_all | solution.py:92
  55.9 0.0 copy-done.6
  55.9 1.6 %copy.65 = bf16[2,256,1,12,128]{4,1,0,3,2:T(8,128)(2,1)} copy(bf16[2,256,1,12,128]{1,4,3,0,2:T(8,128)(2,1)S(1)} %bitcast.49) | data formatting | bytes 3145728 | tf_op jit(solution)/shard_map/all_to_all | solution.py:90
  57.5 2.6 %copy.67 = bf16[2,256,1,12,128]{4,1,0,3,2:T(8,128)(2,1)} copy(bf16[2,256,1,12,128]{1,4,3,0,2:T(8,128)(2,1)} %bitcast.6) | data formatting | bytes 3145728 | tf_op jit(solution)/shard_map/all_to_all | solution.py:91
  60.1 0.0 copy-start.1
  60.1 13.9 %all-to-all-done.2 = bf16[256,2,12,128]{0,3,2,1:T(8,128)(2,1)} async-done(((bf16[256,2,12,128]{0,3,2,1:T(8,128)(2,1)}), bf16[256,2,12,128]{0,3,2,1:T(8,128)(2,1)}, u32[]{:S(2)}, u32[]{:S(2)}) %all-to-all-start.2) | async-done | bytes 1572896 | tf_op jit(solution)/shard_map/all_to_all | solution.py:92
  74.0 2.6 %copy.69 = bf16[2,256,1,12,128]{4,1,0,3,2:T(8,128)(2,1)} copy(bf16[2,256,1,12,128]{1,4,3,0,2:T(8,128)(2,1)} %bitcast.10) | data formatting | bytes 3145728 | tf_op jit(solution)/shard_map/all_to_all | solution.py:92
  76.6 0.0 copy-done.1
  76.6 3.2 %multiply_reduce_fusion = (f32[12,512]{1,0:T(8,128)S(1)}, f32[12,512,512]{1,2,0:T(8,128)S(1)}) fusion(bf16[512,12,128]{2,0,1:T(8,128)(2,1)S(1)} %bitcast.55, bf16[512,12,128]{2,0,1:T(8,128)(2,1)} %bitcast.56), kind=kOutput, calls=%fused_computation.2 | convolution fusion | flops 811591680 | bytes 15753216 | tf_op jit(solution)/shard_map/while/body/eval_jaxpr/qhd,khd->hqk/dot_general | solution.py:42
  79.8 0.0 copy-start.2
  79.8 2.1 %fusion = f32[12,512]{1,0:T(8,128)S(1)} fusion(f32[12,512,512]{1,2,0:T(8,128)S(1)} %get-tuple-element.49, f32[12,512]{1,0:T(8,128)S(1)} %get-tuple-element.48), kind=kLoop, calls=%fused_computation.3 | loop fusion | flops 9431040 | bytes 12632064 | tf_op jit(solution)/shard_map/while/body/eval_jaxpr/reduce_sum | solution.py:46
  81.9 0.0 copy-done.2
  82.0 3.7 %fusion.6 = bf16[512,12,128]{2,0,1:T(8,128)(2,1)S(1)} fusion(bf16[512,12,128]{2,0,1:T(8,128)(2,1)S(1)} %bitcast.58, f32[12,512,512]{1,2,0:T(8,128)S(1)} %get-tuple-element.49, f32[12,512]{1,0:T(8,128)S(1)} %get-tuple-element.48, f32[512,12]{0,1:T(8,128)S(1)} %bitcast.61), kind=kOutput, calls=%fused_computation.9 | convolution fusion | flops 816316416 | bytes 15777792 | tf_op jit(solution)/shard_map/while/body/eval_jaxpr/hqk,khd->qhd/dot_general | solution.py:47
  85.7 1.1 copy.71
  86.8 2.0 %reshape_reshape_broadcast_in_dim_reshape.3 = bf16[8,64,1536]{2,1,0:T(8,128)(2,1)} reshape(bf16[512,12,128]{2,1,0:T(8,128)(2,1)S(1)} %copy.71) | data formatting | bytes 3145728 | tf_op jit(solution)/shard_map/reshape;reshape;broadcast_in_dim;reshape | solution.py:95
  88.8 3.2 %gather_fusion = bf16[8,64,1536]{2,1,0:T(8,128)(2,1)} fusion(bf16[8,64,1536]{2,1,0:T(8,128)(2,1)} %reshape_reshape_broadcast_in_dim_reshape.3, s32[1024]{0:T(1024)S(1)} %pad_clamp_fusion), kind=kCustom, calls=%fused_computation | custom fusion | bytes 3145760 | tf_op jit(solution)/shard_map/gather | solution.py:95
  92.0 2.9 %reshape.57 = bf16[512,1,12,128]{3,2,0,1:T(8,128)(2,1)S(1)} reshape(bf16[8,64,1536]{2,1,0:T(8,128)(2,1)} %gather_fusion) | data formatting | bytes 3145728 | tf_op jit(solution)/shard_map/reshape | solution.py:96
  94.9 25.3 %all_to_all.60 = bf16[512,1,12,128]{3,2,1,0:T(8,128)(2,1)S(1)} all-to-all(bf16[512,1,12,128]{3,2,1,0:T(8,128)(2,1)S(1)} %bitcast.48), channel_id=1, replica_groups=mesh['roll'=16,'seq'=2] {'seq'}, dimensions={0} | all-to-all | bytes 3145728 | tf_op jit(solution)/shard_map/all_to_all | solution.py:97
  120.1 0.4 copy.73
  120.5 0.0 copy-start.3
  120.6 1.6 %copy.74 = bf16[256,2,1,12,128]{0,4,3,1,2:T(8,128)(2,1)} copy(bf16[256,2,1,12,128]{4,0,1,3,2:T(8,128)(2,1)S(1)} %bitcast.53) | data formatting | bytes 3145728 | tf_op jit(solution)/shard_map/all_to_all | solution.py:97
  122.2 0.0 copy-done.3
  122.2 1.8 %convolution_convert_fusion = bf16[256,64]{0,1:T(8,128)(2,1)S(1)} fusion(bf16[3072,64]{0,1:T(8,128)(2,1)S(1)} %copy-done.3, bf16[256,3072]{0,1:T(8,128)(2,1)} %bitcast.54), kind=kOutput, calls=%fused_computation.13 | convolution fusion | flops 100679680 | bytes 1998848 | tf_op jit(solution)/shard_map/dot_general | solution.py:99
  123.9 0.1 reshape.59
  124.1 0.2 copy.75
  124.3 0.3 reshape.60
  124.6 0.8 collective-permute-start
  125.5 0.0 collective-permute-done
  125.5 0.4 collective-permute-start.1
  125.9 3.4 %collective-permute-done.1 = bf16[4,1,1024]{2,1,0:T(2,128)(2,1)S(1)} collective-permute-done((bf16[4,1,1024]{2,1,0:T(2,128)(2,1)S(1)}, bf16[4,1,1024]{2,1,0:T(2,128)(2,1)S(1)}, u32[]{:S(2)}, u32[]{:S(2)}) %collective-permute-start.1) | collective-permute-done | bytes 8224 | tf_op jit(solution)/shard_map/ppermute | solution.py:29
  129.4 0.1 pad_maximum_fusion
  129.4 0.1 copy.76
  129.5 0.5 reshape.61
  130.0 1.4 pad_slice_fusion.1
  131.4 1.8 %pad_slice_fusion = (bf16[2,8,64,16]{3,2,0,1:T(8,128)(2,1)}, bf16[2,8,64,16]{3,2,0,1:T(8,128)(2,1)}, bf16[2,8,64,16]{3,2,0,1:T(8,128)(2,1)}, bf16[2,8,64,16]{3,2...) fusion(bf16[4,10,64,16]{3,2,0,1:T(8,128)(2,1)S(1)} %reshape.61), kind=kLoop, calls=%fused_computation.30 | loop fusion | bytes 1245184 | tf_op jit(solution)/shard_map/slice | solution.py:60
  133.2 1.2 fusion.14
  134.5 5.9 %concatenate.11 = bf16[2,8,64,432]{3,2,0,1:T(8,128)(2,1)S(1)} concatenate(bf16[2,8,64,16]{3,2,0,1:T(8,128)(2,1)} %get-tuple-element.45, bf16[2,8,64,16]{3,2,0,1:T(8,128)(2,1)} %get-tuple-element.44, bf16[2,8,64,16]{3,2,0,1:T(8,128)(2,1)} %get-tuple-element.20, bf16[2,8,64,16]{3,2,0,1:T(8,128)(2,1)} %get-tuple-element.21, bf16[2,8,64,16]{3,2,0,1:T(8,128)(2,1)} %get-tuple-element.43, ...), dimensions={3} | concatenate | bytes 1769472 | tf_op jit(solution)/shard_map/concatenate | solution.py:65
  140.4 0.0 copy-start.5
  140.4 0.1 copy.77
  140.5 0.0 copy-done
  140.5 0.6 copy-done.5
  141.1 0.0 copy-start.4
  141.1 1.9 %divide_multiply_fusion = (f32[1024,512]{1,0:T(8,128)S(1)}, bf16[1024,512]{1,0:T(8,128)(2,1)}) fusion(f32[512]{0:T(512)S(1)} %copy-done.5, bf16[1024,432]{1,0:T(8,128)(2,1)S(1)} %bitcast.60, bf16[432,512]{1,0:T(8,128)(2,1)S(1)} %copy-done), kind=kOutput, calls=%fused_computation.11 | convolution fusion | flops 456130560 | bytes 4474880 | tf_op jit(solution)/shard_map/dot_general | solution.py:116
  143.0 0.0 copy-start.7
  143.0 0.0 copy-done.4
  143.0 0.2 multiply_reduce_fusion.1
  143.2 4.9 %psum.7 = bf16[4,512]{1,0:T(4,128)(2,1)S(1)} all-reduce(bf16[4,512]{1,0:T(4,128)(2,1)S(1)} %multiply_convert_fusion), channel_id=1, replica_groups=mesh['roll'=16,'seq'=2] {'seq'}, use_global_device_ids=true, to_apply=%region_4.5 | all-reduce | flops 2048 | bytes 8192 | tf_op jit(solution)/shard_map/psum | solution.py:125
  148.2 0.0 copy-done.7
  148.2 0.8 fusion.9
  (9 shorter events, 0.1 us)
Async XLA Ops:
  0.6 139.9 %copy-start = (bf16[432,512]{1,0:T(8,128)(2,1)S(1)}, bf16[432,512]{1,0:T(8,128)(2,1)}, u32[]{:S(2)}) copy-start(bf16[432,512]{1,0:T(8,128)(2,1)} %param.13) | copy-start | bytes 1327108
  3.3 24.4 %all-to-all-start = ((bf16[256,2,12,128]{0,3,2,1:T(8,128)(2,1)}), bf16[256,2,12,128]{0,3,2,1:T(8,128)(2,1)S(1)}, u32[]{:S(2)}, u32[]{:S(2)}) async-start(bf16[256,2,12,128]{0,3,2,1:T(8,128)(2,1)} %bitcast.52), calls=%async_computation | async-start | bytes 3145728 | tf_op jit(solution)/shard_map/all_to_all | solution.py:90
  27.6 23.6 %all-to-all-start.1 = ((bf16[256,2,12,128]{0,3,2,1:T(8,128)(2,1)}), bf16[256,2,12,128]{0,3,2,1:T(8,128)(2,1)}, u32[]{:S(2)}, u32[]{:S(2)}) async-start(bf16[256,2,12,128]{0,3,2,1:T(8,128)(2,1)} %bitcast.51), calls=%async_computation.1 | async-start | bytes 3145728 | tf_op jit(solution)/shard_map/all_to_all | solution.py:91
  34.9 21.1 %copy-start.6 = (s32[8]{0:T(128)S(1)}, s32[8]{0:T(128)}, u32[]{:S(2)}) copy-start(s32[8]{0:T(128)} %param.16) | copy-start | bytes 100
  51.3 22.7 %all-to-all-start.2 = ((bf16[256,2,12,128]{0,3,2,1:T(8,128)(2,1)}), bf16[256,2,12,128]{0,3,2,1:T(8,128)(2,1)}, u32[]{:S(2)}, u32[]{:S(2)}) async-start(bf16[256,2,12,128]{0,3,2,1:T(8,128)(2,1)} %bitcast.50), calls=%async_computation.2 | async-start | bytes 3145728 | tf_op jit(solution)/shard_map/all_to_all | solution.py:92
  60.1 16.5 %copy-start.1 = (bf16[2,256,1,12,128]{4,1,0,3,2:T(8,128)(2,1)S(1)}, bf16[2,256,1,12,128]{4,1,0,3,2:T(8,128)(2,1)}, u32[]{:S(2)}) copy-start(bf16[2,256,1,12,128]{4,1,0,3,2:T(8,128)(2,1)} %copy.65) | copy-start | bytes 4718596
  79.8 2.1 %copy-start.2 = (bf16[2,256,1,12,128]{4,1,0,3,2:T(8,128)(2,1)S(1)}, bf16[2,256,1,12,128]{4,1,0,3,2:T(8,128)(2,1)}, u32[]{:S(2)}) copy-start(bf16[2,256,1,12,128]{4,1,0,3,2:T(8,128)(2,1)} %copy.69) | copy-start | bytes 4718596
  120.5 1.6 %copy-start.3 = (bf16[3072,64]{0,1:T(8,128)(2,1)S(1)}, bf16[3072,64]{0,1:T(8,128)(2,1)}, u32[]{:S(2)}) copy-start(bf16[3072,64]{0,1:T(8,128)(2,1)} %param.12) | copy-start | bytes 1179652
  124.6 0.9 collective-permute-start
  125.5 3.8 %collective-permute-start.1 = (bf16[4,1,1024]{2,1,0:T(2,128)(2,1)S(1)}, bf16[4,1,1024]{2,1,0:T(2,128)(2,1)S(1)}, u32[]{:S(2)}, u32[]{:S(2)}) collective-permute-start(bf16[4,1,1024]{2,1,0:T(2,128)(2,1)S(1)} %broadcast_select_fusion.2), channel_id=1, source_target_pairs={{0,1},{1,0},{2,3},{3,2},{4,5},{5,4},{6,7},{7,6},{8,9},{9,8},{10,11... | collective-permute-start | bytes 24584 | tf_op jit(solution)/shard_map/ppermute | solution.py:29
  140.4 0.7 copy-start.5
  141.1 1.9 %copy-start.4 = (f32[1,2,8,64]{3,2,1,0:T(8,128)S(1)}, f32[1,2,8,64]{3,2,1,0:T(8,128)}, u32[]{:S(2)}) copy-start(f32[1,2,8,64]{3,2,1,0:T(8,128)} %param.15) | copy-start | bytes 12292
  143.0 5.2 %copy-start.7 = (s32[4]{0:T(128)S(1)}, s32[4]{0:T(128)}, u32[]{:S(2)}) copy-start(s32[4]{0:T(128)} %param.17) | copy-start | bytes 52
where the time goes:
time: 150 us; the launch traced here: 149 us
  waiting for transfers between devices  51.3 us (34%)
  local copies, waits for them, and re-layouts  38 us (25%)
  blocking collectives  30.2 us (20%)
  starting transfers between devices  14.6 us (10%)
  matrix products  11.4 us (8%)
  other arithmetic  2.48 us (2%)
    all_to_all x1, blocking collectives, local(): lax.all_to_all(ordered, 'seq', split_axis=0, concat_axis=1, tiled=True)  25.3 us
    all_to_all x1, waiting for transfers between devices, local(): lax.all_to_all(to_groups(queries), 'seq', split_axis=1, concat_axis=0, ti...  17.6 us
    all_to_all x1, waiting for transfers between devices, local(): lax.all_to_all(to_groups(keys_in), 'seq', split_axis=1, concat_axis=0, ti...  16.4 us
    all_to_all x1, waiting for transfers between devices, local(): lax.all_to_all(to_groups(values_in), 'seq', split_axis=1, concat_axis=0,...  13.9 us
    unnamed x20, local copies, waits for them, and re-layouts  8.43 us
    concatenate x2, local copies, waits for them, and re-layouts, window_columns(): jnp.concatenate(pieces, axis=-1)  6 us
    psum x1, blocking collectives, local(): lax.psum(pooled_term.astype(jnp.bfloat16), 'seq').astype(jnp.float32)  4.95 us
    all_to_all x1, starting transfers between devices, local(): lax.all_to_all(to_groups(values_in), 'seq', split_axis=1, concat_axis=0,...  4.61 us
  transfers between devices with their start and end apart: 5, of which 4 were waited for; matrix products, arithmetic and copies ran while one was open for 6% of the time, Pallas kernels for 0%

commit v1 on v0

--- a/solution.py
+++ b/solution.py
@@ -3,6 +3,8 @@
 import jax
 import jax.numpy as jnp
 from jax import lax
+from jax.experimental import pallas as pl
+from jax.experimental.pallas import tpu as pltpu
 from jax.sharding import PartitionSpec as P
 
 H = 24
@@ -67,7 +69,14 @@
     )
 
 
-def local(
+def picked(blocks, order):
+    count = blocks.shape[0]
+    choose = (order[:, None] == jnp.arange(count, dtype=jnp.int32)[None, :]).astype(jnp.bfloat16)
+    flat = jnp.dot(choose, blocks.reshape(count, -1), preferred_element_type=jnp.float32)
+    return flat.astype(jnp.bfloat16).reshape(blocks.shape)
+
+
+def local_any(
     queries,
     keys_in,
     values_in,
@@ -92,7 +101,7 @@
     value_all = lax.all_to_all(to_groups(values_in), "seq", split_axis=1, concat_axis=0, tiled=True)
     mixed = heads_attention(query_all[:, 0], key_all[:, 0], value_all[:, 0])[:, None]
     flat_heads = mixed.reshape(seq_len, heads_dev * HD)
-    ordered = flat_heads.reshape(4 * group_count, quarter, heads_dev * HD)[tile_block]
+    ordered = picked(flat_heads.reshape(4 * group_count, quarter, heads_dev * HD), tile_block)
     ordered = ordered.reshape(seq_len, 1, heads_dev, HD)
     returned = lax.all_to_all(ordered, "seq", split_axis=0, concat_axis=1, tiled=True)
     tile_heads = returned.reshape(S_DEV, H * HD)
@@ -131,6 +140,261 @@
     return (decoded, policy)
 
 
+SCALE2 = math.log2(math.e) / math.sqrt(HD)
+HALF = S_DEV // 2
+COLG = 3
+GH = H // COLG
+GW = GH * HD
+NT = (((1,), (1,)), ((), ()))
+
+
+def attend_kernel(
+    q_hbm,
+    k_hbm,
+    v_hbm,
+    w_hbm,
+    lat_out,
+    q,
+    k,
+    v,
+    w,
+    q_in,
+    v_t,
+    w_t,
+    own,
+    stat_own,
+    stat_in,
+    ret,
+    ret_in,
+    lat_own,
+    lat_in,
+    load_sem,
+    q_send,
+    q_recv,
+    small_send,
+    small_recv,
+):
+    me = lax.axis_index("seq")
+    other = 1 - me
+    loads = [
+        pltpu.make_async_copy(src, dst, load_sem.at[i])
+        for i, (src, dst) in enumerate(((q_hbm, q), (k_hbm, k), (v_hbm, v), (w_hbm, w)))
+    ]
+    for load in loads:
+        load.start()
+
+    barrier = pltpu.get_barrier_semaphore()
+    pl.semaphore_signal(barrier, inc=1, device_id={"seq": other})
+    pl.semaphore_wait(barrier, 1)
+
+    def query_copy(half, group):
+        rows = pl.ds(half * HALF, HALF)
+        start = group * GW
+        if not isinstance(group, int):
+            start = pl.multiple_of(start, GW)
+        part = (rows, pl.ds(start, GW))
+        return pltpu.make_async_remote_copy(
+            src_ref=q_hbm.at[part],
+            dst_ref=q_in.at[part],
+            send_sem=q_send.at[half * COLG + group],
+            recv_sem=q_recv.at[half * COLG + group],
+            device_id={"seq": other},
+        )
+
+    def small_copy(src, dst, slot):
+        return pltpu.make_async_remote_copy(
+            src_ref=src,
+            dst_ref=dst,
+            send_sem=small_send.at[slot],
+            recv_sem=small_recv.at[slot],
+            device_id={"seq": other},
+        )
+
+    for group in range(COLG):
+        query_copy(0, group).start()
+    for load in loads:
+        load.wait()
+
+    def head_cols(head):
+        return pl.ds(pl.multiple_of(head * HD, HD), HD)
+
+    def softmax(scores):
+        top = jnp.max(scores, axis=0, keepdims=True)
+        expo = jnp.exp2((scores - top) * SCALE2)
+        return expo.astype(jnp.bfloat16), top * SCALE2, jnp.sum(expo, axis=0, keepdims=True)
+
+    def own_group(group, _):
+        tops, totals = [], []
+        for j in range(GH):
+            head = group * GH + j
+            cols = head_cols(head)
+            value_t = v[:, cols].T
+            v_t[head] = value_t
+            w_t[head] = w[cols, :].T
+            scores = lax.dot_general(k[:, cols], q[:, cols], NT, preferred_element_type=jnp.float32)
+            probs, top, total = softmax(scores)
+            own[head] = jnp.dot(value_t, probs, preferred_element_type=jnp.float32)
+            tops.append(top)
+            totals.append(total)
+        heads = pl.ds(pl.multiple_of(group * GH, GH), GH)
+        stat_own[0, heads, :] = jnp.concatenate(tops, axis=0)
+        stat_own[1, heads, :] = jnp.concatenate(totals, axis=0)
+        return 0
+
+    lax.fori_loop(0, COLG, own_group, 0)
+    stat_copy = small_copy(stat_own, stat_in, 0)
+    stat_copy.start()
+    for group in range(COLG):
+        query_copy(1, group).start()
+    stat_copy.wait_recv()
+
+    def share(top, total, top_b, total_b):
+        most = jnp.maximum(top, top_b)
+        mine = jnp.exp2(top - most)
+        return mine / (total * mine + total_b * jnp.exp2(top_b - most))
+
+    def partner_group(half, group, acc):
+        rows = pl.ds(half * HALF, HALF)
+        query_copy(half, group).wait_recv()
+        first = group * GH if isinstance(group, int) else pl.multiple_of(group * GH, GH)
+        heads = pl.ds(first, GH)
+        tops_b = stat_in[0, heads, rows]
+        totals_b = stat_in[1, heads, rows]
+        tops, totals = [], []
+        for j in range(GH):
+            head = group * GH + j
+            cols = head_cols(head)
+            scores = lax.dot_general(
+                k[:, cols], q_in[rows, cols], NT, preferred_element_type=jnp.float32
+            )
+            probs, top, total = softmax(scores)
+            mixed = jnp.dot(v_t[head], probs, preferred_element_type=jnp.float32)
+            part = share(top, total, tops_b[j : j + 1], totals_b[j : j + 1])
+            acc = acc + jnp.dot(
+                w_t[head], (mixed * part).astype(jnp.bfloat16), preferred_element_type=jnp.float32
+            )
+            tops.append(top)
+            totals.append(total)
+        ret[half, pl.ds(4 * LC + first, GH), :] = jnp.concatenate(tops, axis=0)
+        ret[half, pl.ds(4 * LC + H + first, GH), :] = jnp.concatenate(totals, axis=0)
+        return acc
+
+    ret_copies = [small_copy(ret.at[half], ret_in.at[half], 1 + half) for half in range(2)]
+    lat_copies = [small_copy(lat_own.at[half], lat_in.at[half], 3 + half) for half in range(2)]
+
+    def send_ret(half, acc):
+        ret[half, : 4 * LC, :] = acc
+        ret_copies[half].start()
+
+    def finish(half):
+        rows = pl.ds(half * HALF, HALF)
+        ret_copies[half].wait_recv()
+        part = share(
+            stat_own[0, :, rows],
+            stat_own[1, :, rows],
+            ret_in[half, 4 * LC : 4 * LC + H, :],
+            ret_in[half, 4 * LC + H :, :],
+        )
+        acc = ret_in[half, : 4 * LC, :]
+        for head in range(H):
+            acc = acc + jnp.dot(
+                w_t[head],
+                (own[head, :, rows] * part[head : head + 1]).astype(jnp.bfloat16),
+                preferred_element_type=jnp.float32,
+            )
+        lat_own[half] = acc.astype(jnp.bfloat16)
+        lat_copies[half].start()
+        lat_out[me, half] = lat_own[half]
+
+    zero = jnp.zeros((4 * LC, HALF), jnp.float32)
+    acc = lax.fori_loop(0, COLG, lambda g, a: partner_group(0, g, a), zero)
+    send_ret(0, acc)
+    acc = partner_group(1, 0, zero)
+    finish(0)
+    acc = lax.fori_loop(1, COLG, lambda g, a: partner_group(1, g, a), acc)
+    send_ret(1, acc)
+    finish(1)
+    for half in range(2):
+        lat_copies[half].wait_recv()
+        lat_out[other, half] = lat_in[half]
+    for half in range(2):
+        for group in range(COLG):
+            query_copy(half, group).wait_send()
+    for copy in [stat_copy, *ret_copies, *lat_copies]:
+        copy.wait_send()
+
+
+def attend(queries, keys_in, values_in, latent_proj):
+    width = H * HD
+    any_spec = pl.BlockSpec(memory_space=pl.ANY)
+    bf16, f32 = jnp.bfloat16, jnp.float32
+    return pl.pallas_call(
+        attend_kernel,
+        out_shape=jax.ShapeDtypeStruct((2, 2, 4 * LC, HALF), bf16),
+        in_specs=[any_spec] * 4,
+        out_specs=pl.BlockSpec(memory_space=pltpu.VMEM),
+        scratch_shapes=[
+            pltpu.VMEM((S_DEV, width), bf16),
+            pltpu.VMEM((S_DEV, width), bf16),
+            pltpu.VMEM((S_DEV, width), bf16),
+            pltpu.VMEM((width, 4 * LC), bf16),
+            pltpu.VMEM((S_DEV, width), bf16),
+            pltpu.VMEM((H, HD, S_DEV), bf16),
+            pltpu.VMEM((H, 4 * LC, HD), bf16),
+            pltpu.VMEM((H, HD, S_DEV), f32),
+            pltpu.VMEM((2, H, S_DEV), f32),
+            pltpu.VMEM((2, H, S_DEV), f32),
+            pltpu.VMEM((2, 4 * LC + 2 * H, HALF), f32),
+            pltpu.VMEM((2, 4 * LC + 2 * H, HALF), f32),
+            pltpu.VMEM((2, 4 * LC, HALF), bf16),
+            pltpu.VMEM((2, 4 * LC, HALF), bf16),
+            pltpu.SemaphoreType.DMA((4,)),
+            pltpu.SemaphoreType.DMA((2 * COLG,)),
+            pltpu.SemaphoreType.DMA((2 * COLG,)),
+            pltpu.SemaphoreType.DMA((5,)),
+            pltpu.SemaphoreType.DMA((5,)),
+        ],
+        compiler_params=pltpu.CompilerParams(
+            collective_id=0, has_side_effects=True, vmem_limit_bytes=56 * 2**20
+        ),
+    )(queries, keys_in, values_in, latent_proj)
+
+
+def local_pair(
+    queries,
+    keys_in,
+    values_in,
+    latent_proj,
+    conv_weight,
+    conv_bias,
+    pool_weight,
+    tile_block,
+    owner_slot,
+):
+    my_index = lax.axis_index("seq")
+    lat = attend(queries, keys_in, values_in, latent_proj)
+    tokens = lat.transpose(0, 1, 3, 2).reshape(8, S_DEV // 4, 4 * LC)
+    blocks = picked(tokens, tile_block).reshape(2, FT, RT, WT, 2, 2, LC)
+    video = blocks.transpose(1, 0, 2, 4, 3, 5, 6).reshape(FT, 2 * RL, COLS, LC)
+    volume = jnp.pad(video, ((2, 0), (1, 1), (1, 1), (0, 0)))
+    volume = lax.dynamic_slice_in_dim(volume, my_index * RL, RL + 2, axis=1)
+    pre_act = (
+        jnp.dot(window_columns(volume), conv_weight, preferred_element_type=jnp.float32) + conv_bias
+    )
+    decoded = pre_act.astype(jnp.bfloat16).reshape(1, FT, RL, COLS, CO)
+    weighted = jax.nn.silu(pre_act).reshape(FT, RL, COLS, CO) * pool_weight[0][..., None]
+    pooled_term = jnp.sum(weighted, axis=(0, 1)).reshape(4, COLS // 4, CO).sum(axis=1) / math.sqrt(
+        2 * FT * RL * COLS // 4
+    )
+    total_pooled = lax.psum(pooled_term.astype(jnp.bfloat16), "seq").astype(jnp.float32)
+    wanted_rows = my_index * BPD + jnp.arange(BPD, dtype=jnp.int32)
+    chooser = (owner_slot[None, :] == wanted_rows[:, None]).astype(jnp.float32)
+    policy = jnp.dot(
+        chooser, total_pooled, precision=lax.Precision.HIGHEST, preferred_element_type=jnp.float32
+    )
+    return (decoded, policy)
+
+
 def solution(mesh):
     placed = (
         P(("roll", "seq"), None),
@@ -144,7 +408,7 @@
         P("roll"),
     )
     return jax.shard_map(
-        local,
+        local_pair if mesh.shape["seq"] == 2 else local_any,
         mesh=mesh,
         in_specs=placed,
         out_specs=(P(("roll", "seq"), None, None, None, None), P(("roll", "seq"), None)),

time: 150 us -> 77.4 us (0.52)
  waiting for transfers between devices: 51.3 us -> 0 us
  Pallas kernels: 0 us -> 50.3 us
  blocking collectives: 30.2 us -> 4.95 us
  local copies, waits for them, and re-layouts: 38 us -> 16.2 us
  starting transfers between devices: 14.6 us -> 0 us
  matrix products: 11.4 us -> 4.11 us
  other arithmetic: 2.48 us -> 0.25 us
    pallas_call x0 -> x1, Pallas kernels: none -> 50.3 us  [attend(): pl.pallas_call(attend_kernel, out_shape=jax.ShapeDtypeStruct((2, 2, 4 * L...]
    all_to_all x3 -> x0, waiting for transfers between devices: 47.9 us -> none  [the longest x1 17.6 us: local(): lax.all_to_all(to_groups(queries), 'seq', split_axis=1, concat_axis=0, ti...]
    all_to_all x1 -> x0, blocking collectives: 25.3 us -> none  [local(): lax.all_to_all(ordered, 'seq', split_axis=0, concat_axis=1, tiled=True)]
    all_to_all x3 -> x0, starting transfers between devices: 13.4 us -> none  [the longest x1 4.61 us: local(): lax.all_to_all(to_groups(values_in), 'seq', split_axis=1, concat_axis=0,...]
    all_to_all x5 -> x0, local copies, waits for them, and re-layouts: 8.76 us -> none  [the longest x1 2.6 us: local(): lax.all_to_all(to_groups(values_in), 'seq', split_axis=1, concat_axis=0,...]
    dot_general x5 -> x3, matrix products: 11.4 us -> 4.11 us  [the longest x1 3.13 us: local_pair(): jnp.dot(window_columns(volume), conv_weight, preferred_element_type=jnp.f...]
    unnamed x20 -> x11, local copies, waits for them, and re-layouts: 8.43 us -> 2.23 us
    reshape x5 -> x0, local copies, waits for them, and re-layouts: 3.98 us -> none  [the longest x1 2.89 us: local(): ordered = ordered.reshape(seq_len, 1, heads_dev, HD)]
  transfers between devices with their start and end apart: 5 -> 0, of which waited for: 4 -> 0; matrix products, arithmetic and copies ran while one was open for 6% -> 0% of each run, Pallas kernels for 0% -> 0%
where the time goes in v1:
time: 77.4 us; the launch traced here: 76.5 us
  Pallas kernels  50.3 us (65%)
  local copies, waits for them, and re-layouts  16.2 us (21%)
  blocking collectives  4.95 us (6%)
  matrix products  4.11 us (5%)
    pallas_call x1, Pallas kernels, attend(): pl.pallas_call(attend_kernel, out_shape=jax.ShapeDtypeStruct((2, 2, 4 * L...  50.3 us
    concatenate x1, local copies, waits for them, and re-layouts, window_columns(): jnp.concatenate(pieces, axis=-1)  6.7 us
    slice x2, local copies, waits for them, and re-layouts, window_columns(): volume[a:a + frame_count, b:b + row_count, c:c + col_count]  5.23 us
    psum x1, blocking collectives, local_pair(): lax.psum(pooled_term.astype(jnp.bfloat16), 'seq').astype(jnp.float32)  4.95 us
    dot_general x1, matrix products, local_pair(): jnp.dot(window_columns(volume), conv_weight, preferred_element_type=jnp.f...  3.13 us
    unnamed x11, local copies, waits for them, and re-layouts  2.23 us

profile of v1, /device:TPU:0, one launch (start us, length us, event | category | flops | bytes accessed | tf_op | source)
XLA Modules:
  0.0 76.5 jit_solution(14267436562836907198)
XLA Ops:
  0.6 0.0 copy-start
  0.7 2.2 %copy.15.w_hbm = bf16[3072,64]{1,0:T(8,128)(2,1)} copy(bf16[3072,64]{0,1:T(8,128)(2,1)} %param.12) | data formatting | bytes 786432 | tf_op args[3]
  2.9 0.0 copy-start.2
  2.9 50.3 %shard_map.104 = bf16[2,2,64,128]{3,2,1,0:T(8,128)(2,1)} custom-call(bf16[256,3072]{1,0:T(8,128)(2,1)} %q_hbm.1, bf16[256,3072]{1,0:T(8,128)(2,1)} %k_hbm.1, bf16[256,3072]{1,0:T(8,128)(2,1)} %v_hbm.1, bf16[3072,64]{1,0:T(8,128)(2,1)} %copy.15.w_hbm), custom_call_target="tpu_custom_call" | custom-call | tf_op jit(solution)/shard_map/pallas_call | solution.py:331
  53.2 1.0 %copy.16 = bf16[2,2,128,64]{3,2,1,0:T(8,128)(2,1)S(1)} copy(bf16[2,2,128,64]{2,3,1,0:T(8,128)(2,1)} %bitcast.20) | data formatting | bytes 131072 | tf_op jit(solution)/shard_map/transpose | solution.py:376
  54.1 0.2 reshape_reshape.6
  54.3 0.0 copy-done.2
  54.3 0.2 convolution_convert_fusion
  54.5 0.4 reshape_reshape.7
  55.0 0.5 copy.17
  55.4 2.8 %pad_dynamic-slice_fusion.1 = (bf16[2,8,64,16]{3,2,1,0:T(8,128)(2,1)}, bf16[2,8,64,16]{3,2,1,0:T(8,128)(2,1)}, bf16[2,8,64,16]{3,2,1,0:T(8,128)(2,1)}, bf16[2,8,...) fusion(s32[]{:T(128)S(6)} %add.36, s32[]{:T(128)S(6)} %add.42, ...), kind=kLoop, calls=%fused_computation.1 | loop fusion | bytes 491540 | tf_op jit(solution)/shard_map/slice | solution.py:62
  58.2 2.4 %pad_dynamic-slice_fusion.26 = (bf16[2,8,64,16]{3,2,1,0:T(8,128)(2,1)S(1)}, bf16[2,8,64,16]{3,2,1,0:T(8,128)(2,1)S(1)}, bf16[2,8,64,16]{3,2,1,0:T(8,128)(2,1)S(1...) fusion(s32[]{:T(128)S(6)} %add.36, s32[]{:T(128)S(6)} %add.42, ...), kind=kLoop, calls=%fused_computation.26 | loop fusion | bytes 524308 | tf_op jit(solution)/shard_map/slice | solution.py:62
  60.7 0.0 copy-start.3
  60.7 6.7 %concatenate.3 = bf16[2,8,64,432]{3,2,1,0:T(8,128)(2,1)} concatenate(bf16[2,8,64,16]{3,2,1,0:T(8,128)(2,1)S(1)} %get-tuple-element.5, bf16[2,8,64,16]{3,2,1,0:T(8,128)(2,1)S(1)} %get-tuple-element.6, bf16[2,8,64,16]{3,2,1,0:T(8,128)(2,1)} %get-tuple-element.30, bf16[2,8,64,16]{3,2,1,0:T(8,128)(2,1)S(1)} %get-tuple-element.7, bf16[2,8,64,16]{3,2,1,0:T(8,128)(2,1)S(1)} %get-tuple-element.8, ...), dimensions={3} | concatenate | bytes 1769472 | tf_op jit(solution)/shard_map/concatenate | solution.py:67
  67.4 0.0 copy-done
  67.4 0.0 copy-done.3
  67.4 0.0 copy-start.1
  67.4 3.1 %divide_multiply_fusion = (f32[1024,512]{1,0:T(8,128)S(1)}, bf16[1024,512]{1,0:T(8,128)(2,1)}) fusion(f32[512]{0:T(512)S(1)} %copy-done.3, bf16[1024,432]{1,0:T(8,128)(2,1)} %bitcast.19, bf16[432,512]{1,0:T(8,128)(2,1)S(1)} %copy-done), kind=kOutput, calls=%fused_computation.29 | convolution fusion | flops 456130560 | bytes 4474880 | tf_op jit(solution)/shard_map/dot_general | solution.py:382
  70.5 0.0 copy-start.4
  70.5 0.0 copy-done.1
  70.5 0.2 multiply_reduce_fusion
  70.8 4.9 %psum.7 = bf16[4,512]{1,0:T(4,128)(2,1)S(1)} all-reduce(bf16[4,512]{1,0:T(4,128)(2,1)S(1)} %multiply_convert_fusion), channel_id=1, replica_groups=mesh['roll'=16,'seq'=2] {'seq'}, use_global_device_ids=true, to_apply=%region_2.3 | all-reduce | flops 2048 | bytes 8192 | tf_op jit(solution)/shard_map/psum | solution.py:389
  75.8 0.0 copy-done.4
  75.8 0.8 %fusion.1 = f32[2,512]{1,0:T(2,128)} fusion(bf16[4,512]{1,0:T(4,128)(2,1)S(1)} %psum.7, s32[4]{0:T(128)S(1)} %copy-done.4, s32[2]{0:T(128)S(1)} %iota_add_fusion), kind=kOutput, calls=%fused_computation.35 | convolution fusion | flops 8200 | bytes 8216 | tf_op jit(solution)/shard_map/dot_general | solution.py:392
  (3 shorter events, 0.0 us)
Async XLA Ops:
  0.6 66.8 %copy-start = (bf16[432,512]{1,0:T(8,128)(2,1)S(1)}, bf16[432,512]{1,0:T(8,128)(2,1)}, u32[]{:S(2)}) copy-start(bf16[432,512]{1,0:T(8,128)(2,1)} %param.13) | copy-start | bytes 1327108
  2.9 51.5 %copy-start.2 = (s32[8]{0:T(128)S(1)}, s32[8]{0:T(128)}, u32[]{:S(2)}) copy-start(s32[8]{0:T(128)} %param.16) | copy-start | bytes 100
  60.7 6.7 %copy-start.3 = (f32[512]{0:T(512)S(1)}, f32[512]{0:T(512)}, u32[]{:S(2)}) copy-start(f32[512]{0:T(512)} %param.14) | copy-start | bytes 6148
  67.4 3.1 %copy-start.1 = (f32[1,2,8,64]{3,2,1,0:T(8,128)S(1)}, f32[1,2,8,64]{3,2,1,0:T(8,128)}, u32[]{:S(2)}) copy-start(f32[1,2,8,64]{3,2,1,0:T(8,128)} %param.15) | copy-start | bytes 12292
  70.5 5.2 %copy-start.4 = (s32[4]{0:T(128)S(1)}, s32[4]{0:T(128)}, u32[]{:S(2)}) copy-start(s32[4]{0:T(128)} %param.17) | copy-start | bytes 52

commit v2 on v1

--- a/solution.py
+++ b/solution.py
@@ -153,7 +153,9 @@
     k_hbm,
     v_hbm,
     w_hbm,
+    pool,
     lat_out,
+    pool_out,
     q,
     k,
     v,
@@ -168,6 +170,7 @@
     ret_in,
     lat_own,
     lat_in,
+    pool_in,
     load_sem,
     q_send,
     q_recv,
@@ -230,7 +233,7 @@
             cols = head_cols(head)
             value_t = v[:, cols].T
             v_t[head] = value_t
-            w_t[head] = w[cols, :].T
+            w_t[head] = w[:, cols]
             scores = lax.dot_general(k[:, cols], q[:, cols], NT, preferred_element_type=jnp.float32)
             probs, top, total = softmax(scores)
             own[head] = jnp.dot(value_t, probs, preferred_element_type=jnp.float32)
@@ -244,6 +247,9 @@
     lax.fori_loop(0, COLG, own_group, 0)
     stat_copy = small_copy(stat_own, stat_in, 0)
     stat_copy.start()
+    pool_copy = small_copy(pool, pool_in, 5)
+    pool_copy.start()
+    pool_out[me] = pool[...]
     for group in range(COLG):
         query_copy(1, group).start()
     stat_copy.wait_recv()
@@ -314,30 +320,35 @@
     acc = lax.fori_loop(1, COLG, lambda g, a: partner_group(1, g, a), acc)
     send_ret(1, acc)
     finish(1)
+    pool_copy.wait_recv()
+    pool_out[other] = pool_in[...]
     for half in range(2):
         lat_copies[half].wait_recv()
         lat_out[other, half] = lat_in[half]
     for half in range(2):
         for group in range(COLG):
             query_copy(half, group).wait_send()
-    for copy in [stat_copy, *ret_copies, *lat_copies]:
+    for copy in [stat_copy, pool_copy, *ret_copies, *lat_copies]:
         copy.wait_send()
 
 
-def attend(queries, keys_in, values_in, latent_proj):
+def attend(queries, keys_in, values_in, latent_proj, pool_weight):
     width = H * HD
     any_spec = pl.BlockSpec(memory_space=pl.ANY)
     bf16, f32 = jnp.bfloat16, jnp.float32
     return pl.pallas_call(
         attend_kernel,
-        out_shape=jax.ShapeDtypeStruct((2, 2, 4 * LC, HALF), bf16),
-        in_specs=[any_spec] * 4,
-        out_specs=pl.BlockSpec(memory_space=pltpu.VMEM),
+        out_shape=[
+            jax.ShapeDtypeStruct((2, 2, 4 * LC, HALF), bf16),
+            jax.ShapeDtypeStruct((2, 8, HALF), f32),
+        ],
+        in_specs=[any_spec] * 4 + [pl.BlockSpec(memory_space=pltpu.VMEM)],
+        out_specs=[pl.BlockSpec(memory_space=pltpu.VMEM)] * 2,
         scratch_shapes=[
             pltpu.VMEM((S_DEV, width), bf16),
             pltpu.VMEM((S_DEV, width), bf16),
             pltpu.VMEM((S_DEV, width), bf16),
-            pltpu.VMEM((width, 4 * LC), bf16),
+            pltpu.VMEM((4 * LC, width), bf16),
             pltpu.VMEM((S_DEV, width), bf16),
             pltpu.VMEM((H, HD, S_DEV), bf16),
             pltpu.VMEM((H, 4 * LC, HD), bf16),
@@ -348,16 +359,115 @@
             pltpu.VMEM((2, 4 * LC + 2 * H, HALF), f32),
             pltpu.VMEM((2, 4 * LC, HALF), bf16),
             pltpu.VMEM((2, 4 * LC, HALF), bf16),
+            pltpu.VMEM((8, HALF), f32),
             pltpu.SemaphoreType.DMA((4,)),
             pltpu.SemaphoreType.DMA((2 * COLG,)),
             pltpu.SemaphoreType.DMA((2 * COLG,)),
-            pltpu.SemaphoreType.DMA((5,)),
-            pltpu.SemaphoreType.DMA((5,)),
+            pltpu.SemaphoreType.DMA((6,)),
+            pltpu.SemaphoreType.DMA((6,)),
         ],
         compiler_params=pltpu.CompilerParams(
             collective_id=0, has_side_effects=True, vmem_limit_bytes=56 * 2**20
         ),
-    )(queries, keys_in, values_in, latent_proj)
+    )(queries, keys_in, values_in, latent_proj.T, pool_weight.reshape(8, HALF))
+
+
+def decode_kernel(
+    lat, weight, bias, pool, tile_block, owner_slot, dec_hbm, policy, tok, vol, patch, dec, sem
+):
+    me = lax.axis_index("seq")
+    f32, bf16 = jnp.float32, jnp.bfloat16
+    for part in range(2):
+        for half in range(2):
+            first = (part * 2 + half) * HALF
+            tok[first : first + HALF, :] = lat[part, half].astype(f32).T
+
+    rows, width = 2 * RL, 3 * LC
+    vol[:, :1] = jnp.zeros((FT, 1, COLS + 16, LC), f32)
+    vol[:, rows + 1 :] = jnp.zeros((FT, 1, COLS + 16, LC), f32)
+    vol[:, :, :8] = jnp.zeros((FT, rows + 2, 8, LC), f32)
+    vol[:, :, COLS + 8 :] = jnp.zeros((FT, rows + 2, 8, LC), f32)
+    patch[:2] = jnp.zeros((2, rows, COLS, 3 * width), bf16)
+    for place in range(8):
+        tile, frame, pair = place // 4, place // 2 % 2, place % 2
+        first = tile_block[place] * (2 * WT)
+        for j in range(2):
+            values = tok[pl.ds(pl.multiple_of(first + j * WT, WT), WT), :]
+            for dy in range(2):
+                row = 1 + tile * RL + (pair * 2 + j) * 2 + dy
+                for dx in range(2):
+                    lanes = (dy * 2 + dx) * LC
+                    vol[frame, row, pl.ds(8 + dx, WT, stride=2), :] = values[:, lanes : lanes + LC]
+
+    for frame in range(FT):
+        spans = []
+        for row in range(rows + 2):
+            spans.append(
+                jnp.concatenate(
+                    [vol[frame, row, 7 + c : 7 + c + COLS, :] for c in range(3)], axis=-1
+                ).astype(bf16)
+            )
+        for row in range(rows):
+            patch[frame + 2, row] = jnp.concatenate(spans[row : row + 3], axis=-1)
+
+    lane = lax.broadcasted_iota(jnp.int32, (8, RL * COLS), 1)
+    line = lax.broadcasted_iota(jnp.int32, (8, RL * COLS), 0)
+    in_band = (lane % COLS) // (COLS // 4) == line % 4
+    high_line = line < 4
+    pooled = jnp.zeros((8, CO), f32)
+    out_copy = pltpu.make_async_copy(dec, dec_hbm, sem)
+    for turn in range(2):
+        tile = me if turn == 0 else 1 - me
+        tile_rows = pl.ds(pl.multiple_of(tile * RL, RL), RL)
+        for frame in range(FT):
+            pre = bias[...]
+            for a in range(3):
+                pre = pre + jnp.dot(
+                    patch[frame + a, tile_rows].reshape(RL * COLS, 3 * width),
+                    weight[a * 3 * width : (a + 1) * 3 * width, :],
+                    preferred_element_type=f32,
+                )
+            if turn == 0:
+                dec[0, frame] = pre.astype(bf16).reshape(RL, COLS, CO)
+            act = (0.5 * pre) * (1.0 + jnp.tanh(0.5 * pre))
+            own = jnp.concatenate(
+                [pool[tile, frame * 4 + i : frame * 4 + i + 1, :] for i in range(4)], axis=-1
+            )
+            high = own.astype(bf16).astype(f32)
+            terms = jnp.where(in_band, jnp.where(high_line, high, own - high), 0.0)
+            pooled = pooled + jnp.dot(
+                terms.astype(bf16), act.astype(bf16), preferred_element_type=f32
+            )
+        if turn == 0:
+            out_copy.start()
+    total = (pooled[:4] + pooled[4:]) * (1.0 / math.sqrt(2 * FT * RL * COLS // 4))
+    for i in range(BPD):
+        line_out = jnp.zeros((1, CO), f32)
+        for band in range(4):
+            line_out = jnp.where(owner_slot[band] == me * BPD + i, total[band : band + 1], line_out)
+        policy[i : i + 1, :] = line_out
+    out_copy.wait()
+
+
+def decode(lat, conv_weight, conv_bias, pool, tile_block, owner_slot):
+    vmem = pl.BlockSpec(memory_space=pltpu.VMEM)
+    smem = pl.BlockSpec(memory_space=pltpu.SMEM)
+    bf16, f32 = jnp.bfloat16, jnp.float32
+    dec_shape = (1, FT, RL, COLS, CO)
+    return pl.pallas_call(
+        decode_kernel,
+        out_shape=[jax.ShapeDtypeStruct(dec_shape, bf16), jax.ShapeDtypeStruct((BPD, CO), f32)],
+        in_specs=[vmem] * 4 + [smem] * 2,
+        out_specs=[pl.BlockSpec(memory_space=pl.ANY), vmem],
+        scratch_shapes=[
+            pltpu.VMEM((2 * S_DEV, 4 * LC), f32),
+            pltpu.VMEM((FT, 2 * RL + 2, COLS + 16, LC), f32),
+            pltpu.VMEM((FT + 2, 2 * RL, COLS, 9 * LC), bf16),
+            pltpu.VMEM(dec_shape, bf16),
+            pltpu.SemaphoreType.DMA,
+        ],
+        compiler_params=pltpu.CompilerParams(vmem_limit_bytes=48 * 2**20),
+    )(lat, conv_weight, conv_bias.reshape(1, CO), pool, tile_block, owner_slot)
 
 
 def local_pair(
@@ -371,27 +481,8 @@
     tile_block,
     owner_slot,
 ):
-    my_index = lax.axis_index("seq")
-    lat = attend(queries, keys_in, values_in, latent_proj)
-    tokens = lat.transpose(0, 1, 3, 2).reshape(8, S_DEV // 4, 4 * LC)
-    blocks = picked(tokens, tile_block).reshape(2, FT, RT, WT, 2, 2, LC)
-    video = blocks.transpose(1, 0, 2, 4, 3, 5, 6).reshape(FT, 2 * RL, COLS, LC)
-    volume = jnp.pad(video, ((2, 0), (1, 1), (1, 1), (0, 0)))
-    volume = lax.dynamic_slice_in_dim(volume, my_index * RL, RL + 2, axis=1)
-    pre_act = (
-        jnp.dot(window_columns(volume), conv_weight, preferred_element_type=jnp.float32) + conv_bias
-    )
-    decoded = pre_act.astype(jnp.bfloat16).reshape(1, FT, RL, COLS, CO)
-    weighted = jax.nn.silu(pre_act).reshape(FT, RL, COLS, CO) * pool_weight[0][..., None]
-    pooled_term = jnp.sum(weighted, axis=(0, 1)).reshape(4, COLS // 4, CO).sum(axis=1) / math.sqrt(
-        2 * FT * RL * COLS // 4
-    )
-    total_pooled = lax.psum(pooled_term.astype(jnp.bfloat16), "seq").astype(jnp.float32)
-    wanted_rows = my_index * BPD + jnp.arange(BPD, dtype=jnp.int32)
-    chooser = (owner_slot[None, :] == wanted_rows[:, None]).astype(jnp.float32)
-    policy = jnp.dot(
-        chooser, total_pooled, precision=lax.Precision.HIGHEST, preferred_element_type=jnp.float32
-    )
+    lat, pool = attend(queries, keys_in, values_in, latent_proj, pool_weight)
+    decoded, policy = decode(lat, conv_weight, conv_bias, pool, tile_block, owner_slot)
     return (decoded, policy)
 
 

time: 77.4 us -> 60.1 us (0.78)
  local copies, waits for them, and re-layouts: 16.2 us -> 2.9 us
  Pallas kernels: 50.3 us -> 56.2 us
  blocking collectives: 4.95 us -> 0 us
  matrix products: 4.11 us -> 0 us
    concatenate x1 -> x0, local copies, waits for them, and re-layouts: 6.7 us -> none  [window_columns(): jnp.concatenate(pieces, axis=-1)]
    pallas_call x1 -> x2, Pallas kernels: 50.3 us -> 56.2 us  [the longest x1 51.2 us: attend(): pl.pallas_call(attend_kernel, out_shape=[jax.ShapeDtypeStruct((2, 2, 4 *...]
    slice x2 -> x0, local copies, waits for them, and re-layouts: 5.23 us -> none  [window_columns(): volume[a:a + frame_count, b:b + row_count, c:c + col_count]]
    psum x1 -> x0, blocking collectives: 4.95 us -> none  [local_pair(): lax.psum(pooled_term.astype(jnp.bfloat16), 'seq').astype(jnp.float32)]
    dot_general x3 -> x0, matrix products: 4.11 us -> none  [the longest x1 3.13 us: local_pair(): jnp.dot(window_columns(volume), conv_weight, preferred_element_type=jnp.f...]
    transpose x2 -> x0, local copies, waits for them, and re-layouts: 1.44 us -> none  [the longest x1 0.96 us: local_pair(): tokens = lat.transpose(0, 1, 3, 2).reshape(8, S_DEV // 4, 4 * LC)]
    reshape x0 -> x1, local copies, waits for them, and re-layouts: none -> 1.36 us  [attend(): pool_weight.reshape(8, HALF)]
    unnamed x11 -> x12, local copies, waits for them, and re-layouts: 2.23 us -> 1.54 us
where the time goes in v2:
time: 60.1 us; the launch traced here: 59.8 us
  Pallas kernels  56.2 us (94%)
  local copies, waits for them, and re-layouts  2.9 us (5%)
  between operations  0.68 us (1%)
    pallas_call x1, Pallas kernels, attend(): pl.pallas_call(attend_kernel, out_shape=[jax.ShapeDtypeStruct((2, 2, 4 *...  51.2 us
    pallas_call x1, Pallas kernels, decode(): pl.pallas_call(decode_kernel, out_shape=[jax.ShapeDtypeStruct(dec_shape,...  4.97 us
    unnamed x12, local copies, waits for them, and re-layouts  1.54 us
    reshape x1, local copies, waits for them, and re-layouts, attend(): pool_weight.reshape(8, HALF)  1.36 us

profile of v2, /device:TPU:0, one launch (start us, length us, event | category | flops | bytes accessed | tf_op | source)
XLA Modules:
  0.0 59.8 jit_solution(11099678041522868319)
XLA Ops:
  0.6 1.4 %reshape.10.pool = f32[8,128]{1,0:T(8,128)} reshape(f32[1,2,8,64]{3,2,1,0:T(8,128)} %param.15) | data formatting | bytes 8192 | tf_op jit(solution)/shard_map/reshape | solution.py:372
  2.0 0.0 copy-start
  2.0 0.0 copy-start.3
  2.0 0.0 copy-start.4
  2.0 0.0 copy-start.5
  2.0 51.2 %shard_map.104 = (bf16[2,2,64,128]{3,2,1,0:T(8,128)(2,1)}, f32[2,8,128]{2,1,0:T(8,128)}) custom-call(bf16[256,3072]{1,0:T(8,128)(2,1)} %q_hbm.1, bf16[256,3072]{1,0:T(8,128)(2,1)} %k_hbm.1, bf16[256,3072]{1,0:T(8,128)(2,1)} %v_hbm.1, bf16[64,3072]{1,0:T(8,128)(2,1)} %bitcast.5, f32[8,128]{1,0:T(8,128)} %reshape.10.pool), custom_call_target="tpu_custom_call" | custom-call | tf_op jit(solution)/shard_map/pallas_call | solution.py:339
  53.2 0.0 copy-done
  53.2 0.0 copy-done.3
  53.2 0.0 copy-done.4
  53.3 0.0 copy-done.5
  53.3 0.0 copy-start.1
  53.3 0.8 %copy-done.1 = bf16[2,2,64,128]{3,2,1,0:T(8,128)(2,1)S(1)} copy-done((bf16[2,2,64,128]{3,2,1,0:T(8,128)(2,1)S(1)}, bf16[2,2,64,128]{3,2,1,0:T(8,128)(2,1)}, u32[]{:S(2)}) %copy-start.1) | copy-done | bytes 65560
  54.1 0.0 copy-start.2
  54.1 0.7 %copy-done.2 = f32[2,8,128]{2,1,0:T(8,128)S(1)} copy-done((f32[2,8,128]{2,1,0:T(8,128)S(1)}, f32[2,8,128]{2,1,0:T(8,128)}, u32[]{:S(2)}) %copy-start.2) | copy-done | bytes 8216
  54.8 5.0 %shard_map.105 = (bf16[1,2,8,64,512]{4,3,2,1,0:T(8,128)(2,1)}, f32[2,512]{1,0:T(2,128)}) custom-call(bf16[2,2,64,128]{3,2,1,0:T(8,128)(2,1)S(1)} %copy-done.1, bf16[432,512]{1,0:T(8,128)(2,1)S(1)} %copy-done, f32[1,512]{1,0:T(1,128)S(1)} %bitcast.4, f32[2,8,128]{2,1,0:T(8,128)S(1)} %copy-done.2, s32[8]{0:T(128)S(1)} %copy-done.4, s32[4]{0:T(128)S(1)} %copy-done.5), custom_call_target="tpu_custom_call" | custom-call | tf_op jit(solution)/shard_map/pallas_call | solution.py:457
Async XLA Ops:
  2.0 51.2 %copy-start = (bf16[432,512]{1,0:T(8,128)(2,1)S(1)}, bf16[432,512]{1,0:T(8,128)(2,1)}, u32[]{:S(2)}) copy-start(bf16[432,512]{1,0:T(8,128)(2,1)} %weight.1) | copy-start | bytes 1327108
  2.0 51.2 %copy-start.3 = (f32[512]{0:T(512)S(1)}, f32[512]{0:T(512)}, u32[]{:S(2)}) copy-start(f32[512]{0:T(512)} %param.14) | copy-start | bytes 6148
  2.0 51.3 %copy-start.4 = (s32[8]{0:T(128)S(1)}, s32[8]{0:T(128)}, u32[]{:S(2)}) copy-start(s32[8]{0:T(128)} %tile_block.1) | copy-start | bytes 100
  2.0 51.3 %copy-start.5 = (s32[4]{0:T(128)S(1)}, s32[4]{0:T(128)}, u32[]{:S(2)}) copy-start(s32[4]{0:T(128)} %owner_slot.1) | copy-start | bytes 52
  53.3 0.8 %copy-start.1 = (bf16[2,2,64,128]{3,2,1,0:T(8,128)(2,1)S(1)}, bf16[2,2,64,128]{3,2,1,0:T(8,128)(2,1)}, u32[]{:S(2)}) copy-start(bf16[2,2,64,128]{3,2,1,0:T(8,128)(2,1)} %get-tuple-element.4.lat) | copy-start | bytes 196612
  54.1 0.7 %copy-start.2 = (f32[2,8,128]{2,1,0:T(8,128)S(1)}, f32[2,8,128]{2,1,0:T(8,128)}, u32[]{:S(2)}) copy-start(f32[2,8,128]{2,1,0:T(8,128)} %get-tuple-element.5.pool) | copy-start | bytes 24580

commit v3 on v2

--- a/solution.py
+++ b/solution.py
@@ -164,10 +164,13 @@
     v_t,
     w_t,
     own,
+    top_own,
     stat_own,
     stat_in,
     ret,
     ret_in,
+    ret_level,
+    level_in,
     lat_own,
     lat_in,
     pool_in,
@@ -224,10 +227,12 @@
     def softmax(scores):
         top = jnp.max(scores, axis=0, keepdims=True)
         expo = jnp.exp2((scores - top) * SCALE2)
-        return expo.astype(jnp.bfloat16), top * SCALE2, jnp.sum(expo, axis=0, keepdims=True)
+        top = top * SCALE2
+        level = top + jnp.log(jnp.sum(expo, axis=0, keepdims=True)) * math.log2(math.e)
+        return expo.astype(jnp.bfloat16), top, level
 
     def own_group(group, _):
-        tops, totals = [], []
+        tops, levels = [], []
         for j in range(GH):
             head = group * GH + j
             cols = head_cols(head)
@@ -235,13 +240,13 @@
             v_t[head] = value_t
             w_t[head] = w[:, cols]
             scores = lax.dot_general(k[:, cols], q[:, cols], NT, preferred_element_type=jnp.float32)
-            probs, top, total = softmax(scores)
+            probs, top, level = softmax(scores)
             own[head] = jnp.dot(value_t, probs, preferred_element_type=jnp.float32)
             tops.append(top)
-            totals.append(total)
+            levels.append(level)
         heads = pl.ds(pl.multiple_of(group * GH, GH), GH)
-        stat_own[0, heads, :] = jnp.concatenate(tops, axis=0)
-        stat_own[1, heads, :] = jnp.concatenate(totals, axis=0)
+        top_own[heads, :] = jnp.concatenate(tops, axis=0)
+        stat_own[heads, :] = jnp.concatenate(levels, axis=0)
         return 0
 
     lax.fori_loop(0, COLG, own_group, 0)
@@ -254,54 +259,51 @@
         query_copy(1, group).start()
     stat_copy.wait_recv()
 
-    def share(top, total, top_b, total_b):
-        most = jnp.maximum(top, top_b)
-        mine = jnp.exp2(top - most)
-        return mine / (total * mine + total_b * jnp.exp2(top_b - most))
+    def share(top, level, level_b):
+        most = jnp.maximum(level, level_b)
+        both = jnp.exp2(level - most) + jnp.exp2(level_b - most)
+        return jnp.exp2(top - most) / both
 
     def partner_group(half, group, acc):
         rows = pl.ds(half * HALF, HALF)
         query_copy(half, group).wait_recv()
         first = group * GH if isinstance(group, int) else pl.multiple_of(group * GH, GH)
         heads = pl.ds(first, GH)
-        tops_b = stat_in[0, heads, rows]
-        totals_b = stat_in[1, heads, rows]
-        tops, totals = [], []
+        levels_b = stat_in[heads, rows]
+        levels = []
         for j in range(GH):
             head = group * GH + j
             cols = head_cols(head)
             scores = lax.dot_general(
                 k[:, cols], q_in[rows, cols], NT, preferred_element_type=jnp.float32
             )
-            probs, top, total = softmax(scores)
+            probs, top, level = softmax(scores)
             mixed = jnp.dot(v_t[head], probs, preferred_element_type=jnp.float32)
-            part = share(top, total, tops_b[j : j + 1], totals_b[j : j + 1])
+            part = share(top, level, levels_b[j : j + 1])
             acc = acc + jnp.dot(
                 w_t[head], (mixed * part).astype(jnp.bfloat16), preferred_element_type=jnp.float32
             )
-            tops.append(top)
-            totals.append(total)
-        ret[half, pl.ds(4 * LC + first, GH), :] = jnp.concatenate(tops, axis=0)
-        ret[half, pl.ds(4 * LC + H + first, GH), :] = jnp.concatenate(totals, axis=0)
+            levels.append(level)
+        ret_level[half, heads, :] = jnp.concatenate(levels, axis=0)
         return acc
 
     ret_copies = [small_copy(ret.at[half], ret_in.at[half], 1 + half) for half in range(2)]
+    level_copies = [
+        small_copy(ret_level.at[half], level_in.at[half], 6 + half) for half in range(2)
+    ]
     lat_copies = [small_copy(lat_own.at[half], lat_in.at[half], 3 + half) for half in range(2)]
 
     def send_ret(half, acc):
-        ret[half, : 4 * LC, :] = acc
+        level_copies[half].start()
+        ret[half] = acc.astype(jnp.bfloat16)
         ret_copies[half].start()
 
     def finish(half):
         rows = pl.ds(half * HALF, HALF)
+        level_copies[half].wait_recv()
+        part = share(top_own[:, rows], stat_own[:, rows], level_in[half])
         ret_copies[half].wait_recv()
-        part = share(
-            stat_own[0, :, rows],
-            stat_own[1, :, rows],
-            ret_in[half, 4 * LC : 4 * LC + H, :],
-            ret_in[half, 4 * LC + H :, :],
-        )
-        acc = ret_in[half, : 4 * LC, :]
+        acc = ret_in[half].astype(jnp.float32)
         for head in range(H):
             acc = acc + jnp.dot(
                 w_t[head],
@@ -328,7 +330,7 @@
     for half in range(2):
         for group in range(COLG):
             query_copy(half, group).wait_send()
-    for copy in [stat_copy, pool_copy, *ret_copies, *lat_copies]:
+    for copy in [stat_copy, pool_copy, *level_copies, *ret_copies, *lat_copies]:
         copy.wait_send()
 
 
@@ -340,7 +342,7 @@
         attend_kernel,
         out_shape=[
             jax.ShapeDtypeStruct((2, 2, 4 * LC, HALF), bf16),
-            jax.ShapeDtypeStruct((2, 8, HALF), f32),
+            jax.ShapeDtypeStruct((2, FT * RL, COLS), f32),
         ],
         in_specs=[any_spec] * 4 + [pl.BlockSpec(memory_space=pltpu.VMEM)],
         out_specs=[pl.BlockSpec(memory_space=pltpu.VMEM)] * 2,
@@ -353,23 +355,26 @@
             pltpu.VMEM((H, HD, S_DEV), bf16),
             pltpu.VMEM((H, 4 * LC, HD), bf16),
             pltpu.VMEM((H, HD, S_DEV), f32),
-            pltpu.VMEM((2, H, S_DEV), f32),
-            pltpu.VMEM((2, H, S_DEV), f32),
-            pltpu.VMEM((2, 4 * LC + 2 * H, HALF), f32),
-            pltpu.VMEM((2, 4 * LC + 2 * H, HALF), f32),
+            pltpu.VMEM((H, S_DEV), f32),
+            pltpu.VMEM((H, S_DEV), f32),
+            pltpu.VMEM((H, S_DEV), f32),
             pltpu.VMEM((2, 4 * LC, HALF), bf16),
             pltpu.VMEM((2, 4 * LC, HALF), bf16),
-            pltpu.VMEM((8, HALF), f32),
+            pltpu.VMEM((2, H, HALF), f32),
+            pltpu.VMEM((2, H, HALF), f32),
+            pltpu.VMEM((2, 4 * LC, HALF), bf16),
+            pltpu.VMEM((2, 4 * LC, HALF), bf16),
+            pltpu.VMEM((FT * RL, COLS), f32),
             pltpu.SemaphoreType.DMA((4,)),
             pltpu.SemaphoreType.DMA((2 * COLG,)),
             pltpu.SemaphoreType.DMA((2 * COLG,)),
-            pltpu.SemaphoreType.DMA((6,)),
-            pltpu.SemaphoreType.DMA((6,)),
+            pltpu.SemaphoreType.DMA((8,)),
+            pltpu.SemaphoreType.DMA((8,)),
         ],
         compiler_params=pltpu.CompilerParams(
             collective_id=0, has_side_effects=True, vmem_limit_bytes=56 * 2**20
         ),
-    )(queries, keys_in, values_in, latent_proj.T, pool_weight.reshape(8, HALF))
+    )(queries, keys_in, values_in, latent_proj.T, pool_weight.reshape(FT * RL, COLS))
 
 
 def decode_kernel(
@@ -431,7 +436,7 @@
                 dec[0, frame] = pre.astype(bf16).reshape(RL, COLS, CO)
             act = (0.5 * pre) * (1.0 + jnp.tanh(0.5 * pre))
             own = jnp.concatenate(
-                [pool[tile, frame * 4 + i : frame * 4 + i + 1, :] for i in range(4)], axis=-1
+                [pool[tile, frame * RL + i : frame * RL + i + 1, :] for i in range(RL)], axis=-1
             )
             high = own.astype(bf16).astype(f32)
             terms = jnp.where(in_band, jnp.where(high_line, high, own - high), 0.0)
@@ -466,7 +471,7 @@
             pltpu.VMEM(dec_shape, bf16),
             pltpu.SemaphoreType.DMA,
         ],
-        compiler_params=pltpu.CompilerParams(vmem_limit_bytes=48 * 2**20),
+        compiler_params=pltpu.CompilerParams(vmem_limit_bytes=60 * 2**20),
     )(lat, conv_weight, conv_bias.reshape(1, CO), pool, tile_block, owner_slot)
 
 

time: 60.1 us -> 55.8 us (0.928)
  local copies, waits for them, and re-layouts: 2.9 us -> 0 us
  Pallas kernels: 56.2 us -> 55 us
    unnamed x12 -> x0, local copies, waits for them, and re-layouts: 1.54 us -> none
    pallas_call x1, Pallas kernels: 51.2 us -> 49.7 us  [attend(): pl.pallas_call(attend_kernel, out_shape=[jax.ShapeDtypeStruct((2, 2, 4 *...]
    reshape x1 -> x0, local copies, waits for them, and re-layouts: 1.36 us -> none  [attend(): pool_weight.reshape(8, HALF)]
where the time goes in v3:
time: 55.8 us; the launch traced here: 55.6 us
  Pallas kernels  55 us (99%)
  between operations  0.64 us (1%)
    pallas_call x1, Pallas kernels, attend(): pl.pallas_call(attend_kernel, out_shape=[jax.ShapeDtypeStruct((2, 2, 4 *...  49.7 us
    pallas_call x1, Pallas kernels, decode(): pl.pallas_call(decode_kernel, out_shape=[jax.ShapeDtypeStruct(dec_shape,...  5.29 us

profile of v3, /device:TPU:0, one launch (start us, length us, event | category | flops | bytes accessed | tf_op | source)
XLA Modules:
  0.0 55.6 jit_solution(2739911815947894120)
XLA Ops:
  0.6 49.7 %shard_map.104 = (bf16[2,2,64,128]{3,2,1,0:T(8,128)(2,1)}, f32[2,16,64]{2,1,0:T(8,128)}) custom-call(bf16[256,3072]{1,0:T(8,128)(2,1)} %q_hbm.1, bf16[256,3072]{1,0:T(8,128)(2,1)} %k_hbm.1, bf16[256,3072]{1,0:T(8,128)(2,1)} %v_hbm.1, bf16[64,3072]{1,0:T(8,128)(2,1)} %bitcast.3, f32[16,64]{1,0:T(8,128)} %bitcast.4), custom_call_target="tpu_custom_call" | custom-call | tf_op jit(solution)/shard_map/pallas_call | solution.py:341
  50.3 5.3 %shard_map.105 = (bf16[1,2,8,64,512]{4,3,2,1,0:T(8,128)(2,1)}, f32[2,512]{1,0:T(2,128)}) custom-call(bf16[2,2,64,128]{3,2,1,0:T(8,128)(2,1)} %get-tuple-element.4.lat, bf16[432,512]{1,0:T(8,128)(2,1)} %weight.1, f32[1,512]{1,0:T(1,128)} %bitcast.5, f32[2,16,64]{2,1,0:T(8,128)} %get-tuple-element.5.pool, s32[8]{0:T(128)} %tile_block.1, s32[4]{0:T(128)} %owner_slot.1), custom_call_target="tpu_custom_call" | custom-call | tf_op jit(solution)/shard_map/pallas_call | solution.py:462

commit v4 on v3

--- a/solution.py
+++ b/solution.py
@@ -193,17 +193,18 @@
     pl.semaphore_signal(barrier, inc=1, device_id={"seq": other})
     pl.semaphore_wait(barrier, 1)
 
-    def query_copy(half, group):
+    def query_copy(half, group, piece):
         rows = pl.ds(half * HALF, HALF)
-        start = group * GW
+        start = group * GW + piece * (GW // 2)
         if not isinstance(group, int):
-            start = pl.multiple_of(start, GW)
-        part = (rows, pl.ds(start, GW))
+            start = pl.multiple_of(start, GW // 2)
+        slot = (half * COLG + group) * 2 + piece
+        part = (rows, pl.ds(start, GW // 2))
         return pltpu.make_async_remote_copy(
             src_ref=q_hbm.at[part],
             dst_ref=q_in.at[part],
-            send_sem=q_send.at[half * COLG + group],
-            recv_sem=q_recv.at[half * COLG + group],
+            send_sem=q_send.at[slot],
+            recv_sem=q_recv.at[slot],
             device_id={"seq": other},
         )
 
@@ -217,7 +218,8 @@
         )
 
     for group in range(COLG):
-        query_copy(0, group).start()
+        query_copy(0, group, 0).start()
+        query_copy(0, group, 1).start()
     for load in loads:
         load.wait()
 
@@ -256,7 +258,8 @@
     pool_copy.start()
     pool_out[me] = pool[...]
     for group in range(COLG):
-        query_copy(1, group).start()
+        query_copy(1, group, 0).start()
+        query_copy(1, group, 1).start()
     stat_copy.wait_recv()
 
     def share(top, level, level_b):
@@ -266,12 +269,13 @@
 
     def partner_group(half, group, acc):
         rows = pl.ds(half * HALF, HALF)
-        query_copy(half, group).wait_recv()
         first = group * GH if isinstance(group, int) else pl.multiple_of(group * GH, GH)
         heads = pl.ds(first, GH)
         levels_b = stat_in[heads, rows]
         levels = []
         for j in range(GH):
+            if j % (GH // 2) == 0:
+                query_copy(half, group, j // (GH // 2)).wait_recv()
             head = group * GH + j
             cols = head_cols(head)
             scores = lax.dot_general(
@@ -329,7 +333,8 @@
         lat_out[other, half] = lat_in[half]
     for half in range(2):
         for group in range(COLG):
-            query_copy(half, group).wait_send()
+            query_copy(half, group, 0).wait_send()
+            query_copy(half, group, 1).wait_send()
     for copy in [stat_copy, pool_copy, *level_copies, *ret_copies, *lat_copies]:
         copy.wait_send()
 
@@ -366,8 +371,8 @@
             pltpu.VMEM((2, 4 * LC, HALF), bf16),
             pltpu.VMEM((FT * RL, COLS), f32),
             pltpu.SemaphoreType.DMA((4,)),
-            pltpu.SemaphoreType.DMA((2 * COLG,)),
-            pltpu.SemaphoreType.DMA((2 * COLG,)),
+            pltpu.SemaphoreType.DMA((4 * COLG,)),
+            pltpu.SemaphoreType.DMA((4 * COLG,)),
             pltpu.SemaphoreType.DMA((8,)),
             pltpu.SemaphoreType.DMA((8,)),
         ],

time: 55.8 us -> 56.3 us (level)
  no operation moved by 1% of the time
where the time goes in v4:
time: 56.3 us; the launch traced here: 56.1 us
  Pallas kernels  55.5 us (99%)
  between operations  0.64 us (1%)
    pallas_call x1, Pallas kernels, attend(): pl.pallas_call(attend_kernel, out_shape=[jax.ShapeDtypeStruct((2, 2, 4 *...  50.2 us
    pallas_call x1, Pallas kernels, decode(): pl.pallas_call(decode_kernel, out_shape=[jax.ShapeDtypeStruct(dec_shape,...  5.27 us

profile of v4, /device:TPU:0, one launch (start us, length us, event | category | flops | bytes accessed | tf_op | source)
XLA Modules:
  0.0 56.1 jit_solution(12188938887941828253)
XLA Ops:
  0.6 50.2 %shard_map.104 = (bf16[2,2,64,128]{3,2,1,0:T(8,128)(2,1)}, f32[2,16,64]{2,1,0:T(8,128)}) custom-call(bf16[256,3072]{1,0:T(8,128)(2,1)} %q_hbm.1, bf16[256,3072]{1,0:T(8,128)(2,1)} %k_hbm.1, bf16[256,3072]{1,0:T(8,128)(2,1)} %v_hbm.1, bf16[64,3072]{1,0:T(8,128)(2,1)} %bitcast.3, f32[16,64]{1,0:T(8,128)} %bitcast.4), custom_call_target="tpu_custom_call" | custom-call | tf_op jit(solution)/shard_map/pallas_call | solution.py:346
  50.9 5.3 %shard_map.105 = (bf16[1,2,8,64,512]{4,3,2,1,0:T(8,128)(2,1)}, f32[2,512]{1,0:T(2,128)}) custom-call(bf16[2,2,64,128]{3,2,1,0:T(8,128)(2,1)} %get-tuple-element.4.lat, bf16[432,512]{1,0:T(8,128)(2,1)} %weight.1, f32[1,512]{1,0:T(1,128)} %bitcast.5, f32[2,16,64]{2,1,0:T(8,128)} %get-tuple-element.5.pool, s32[8]{0:T(128)} %tile_block.1, s32[4]{0:T(128)} %owner_slot.1), custom_call_target="tpu_custom_call" | custom-call | tf_op jit(solution)/shard_map/pallas_call | solution.py:467
